TPU v7x, 32 devices: a whole 2x2x4 slice. The times are simulated.
32 devices in a mesh: rep: 4 (over y, x), fsdp: 8 (over z, core).
Axes of the slice: x: 2, y: 2, z: 4, core: 2. Of those that a mesh axis runs over, the one named last changes fastest.
Arguments:
- activations: bfloat16 [8192, 512], P(('rep', 'fsdp')), may hold values from -6 to 6
- output_grads: bfloat16 [8192, 8192], P(('rep', 'fsdp'))
- master: float32 [8192, 512], P('fsdp'), may hold values from -6 to 6
- first_moment: float32 [8192, 512], P('fsdp'), may hold values from -4 to 4
- second_moment: float32 [8192, 512], P('fsdp'), may hold values from 0.2 to 2
Outputs:
- new_master: float32 [8192, 512], P('fsdp')
- new_first: float32 [8192, 512], P('fsdp')
- new_second: float32 [8192, 512], P('fsdp')
- params: bfloat16 [8192, 512], replicated
All inputs are finite; a program needn't handle non-finite values.
Results may differ from a plain program's by a relative error of at most 0.0004.
Values may be sent and summed in bfloat16 or wider, within the bound.
A program may use at most 128 MiB of HBM per device.

v0:
```python
import jax
import jax.numpy as jnp
from jax import lax
from jax.sharding import PartitionSpec as P

dot_epsilon = 1e-06
beta_one = 0.9
beta_two = 0.95
adam_epsilon = 1e-08
learn_rate = 0.02
decay_rate = 0.1
contract_first = (((0,), (0,)), ((), ()))


def swapped(shard, axis, apart):
    return lax.ppermute(shard, axis, [(i, i ^ 1 << apart) for i in range(lax.axis_size(axis))])


def reversed_bits(number_in, bit_count):
    result = 0
    for position in range(bit_count):
        result = result << 1 | number_in >> position & 1
    return result


def local(activations, output_grads, master, first_moment, second_moment):
    grad_shard = lax.psum_scatter(
        lax.dot_general(
            output_grads, activations, contract_first, preferred_element_type=jnp.float32
        ),
        "fsdp",
        scatter_dimension=0,
        tiled=True,
    )
    replica_count = lax.axis_size("rep")
    level_total = replica_count.bit_length() - 1
    replica = lax.axis_index("rep")
    current = grad_shard
    for level_index in range(level_total):
        side_bit = replica >> level_index & 1
        low_side = side_bit == 0
        half_rows = current.shape[0] // 2
        lower_half = current[:half_rows]
        upper_half = current[half_rows:]
        kept_rows = jnp.where(low_side, lower_half, upper_half)
        outgoing = jnp.where(low_side, upper_half, lower_half)
        incoming = swapped(outgoing, "rep", level_index)
        left_vec = jnp.where(low_side, kept_rows, incoming)
        right_vec = jnp.where(low_side, incoming, kept_rows)
        partial_dots = jnp.stack(
            [
                jnp.sum(left_vec * right_vec),
                jnp.sum(left_vec * left_vec),
                jnp.sum(right_vec * right_vec),
            ]
        )
        totals = lax.psum(partial_dots, "fsdp")
        for inner_bit in range(level_index + 1):
            totals = totals + swapped(totals, "rep", inner_bit)
        left_coef = 1.0 - totals[0] / (2.0 * (totals[1] + dot_epsilon))
        right_coef = 1.0 - totals[0] / (2.0 * (totals[2] + dot_epsilon))
        current = left_coef * left_vec + right_coef * right_vec
    piece_rows = current.shape[0]
    gathered = lax.all_gather(current, "rep", axis=0, tiled=True)
    ordered = [
        gathered[
            reversed_bits(place, level_total)
            * piece_rows : (reversed_bits(place, level_total) + 1)
            * piece_rows
        ]
        for place in range(replica_count)
    ]
    combined = jnp.concatenate(ordered, axis=0)
    correct_one = 1.0 - (beta_one**50) ** 2
    correct_two = 1.0 - (beta_two**50) ** 2
    new_first = beta_one * first_moment + (1.0 - beta_one) * combined
    new_second = beta_two * second_moment + (1.0 - beta_two) * combined * combined
    update = (
        new_first / correct_one / (jnp.sqrt(new_second / correct_two) + adam_epsilon)
        + decay_rate * master
    )
    new_master = master - learn_rate * update
    params = lax.all_gather(new_master.astype(jnp.bfloat16), "fsdp", axis=0, tiled=True)
    return (new_master, new_first, new_second, params)


def solution(mesh):
    in_specs = (
        P(("rep", "fsdp"), None),
        P(("rep", "fsdp"), None),
        P("fsdp", None),
        P("fsdp", None),
        P("fsdp", None),
    )
    out_specs = (P("fsdp", None), P("fsdp", None), P("fsdp", None), P())
    return jax.shard_map(local, mesh=mesh, in_specs=in_specs, out_specs=out_specs, check_vma=False)
```

profile of v0, /device:TPU:25, one launch (start us, length us, event | category | flops | bytes accessed | tf_op | source)
XLA Modules:
  0.0 414.4 jit_solution(617490550681999594)
XLA Ops:
  8.1 10.3 %fusion.6 = f32[8192,512]{1,0:T(8,128)} fusion(bf16[256,8192]{1,0:T(8,128)(2,1)} %param.6, bf16[256,512]{1,0:T(8,128)(2,1)S(1)} %copy-done), kind=kOutput, calls=%fused_computation.27 | convolution fusion | flops 2147483648 | bytes 21233664 | tf_op jit(solution)/shard_map/dot_general | solution.py:28
  18.5 166.5 %reduce-scatter.2.cloned.1.call-done = f32[1024,512]{1,0:T(8,128)} async-done(((f32[8192,512]{1,0:T(8,128)}), f32[1024,512]{1,0:T(8,128)}) %reduce-scatter.2.cloned.1.call-update) | async-done | bytes 2097168 | tf_op jit(solution)/shard_map/reduce_scatter | solution.py:27
  185.0 1.9 slice_select_fusion
  186.9 1.5 collective-permute-start
  188.4 22.4 %collective-permute-done = f32[512,512]{1,0:T(8,128)} collective-permute-done((f32[512,512]{1,0:T(8,128)S(1)}, f32[512,512]{1,0:T(8,128)}, u32[]{:S(2)}, u32[]{:S(2)}) %collective-permute-start) | collective-permute-done | bytes 1048608 | tf_op jit(solution)/shard_map/ppermute | solution.py:16
  210.7 3.1 multiply_reduce_fusion.2
  213.8 2.0 pad_maximum_fusion.1
  215.9 13.0 %psum.14 = f32[3]{0:T(128)S(1)} all-reduce(f32[3]{0:T(128)S(1)} %pad_maximum_fusion.1), channel_id=1, replica_groups=mesh['rep'=4,'fsdp'=8] {'fsdp'}, use_global_device_ids=true, to_apply=%region_4.5 | all-reduce | flops 3 | bytes 24 | tf_op jit(solution)/shard_map/psum | solution.py:57
  228.9 1.8 collective-permute-start.1
  230.7 0.9 collective-permute-done.1
  234.8 1.5 multiply_add_fusion.1
  236.4 1.6 collective-permute-start.2
  238.0 10.8 %collective-permute-done.2 = f32[256,512]{1,0:T(8,128)S(1)} collective-permute-done((f32[256,512]{1,0:T(8,128)S(1)}, f32[256,512]{1,0:T(8,128)S(1)}, u32[]{:S(2)}, u32[]{:S(2)}) %collective-permute-start.2) | collective-permute-done | bytes 524320 | tf_op jit(solution)/shard_map/ppermute | solution.py:16
  249.7 2.0 pad_maximum_fusion.2
  251.7 13.8 %psum.15 = f32[3]{0:T(128)S(1)} all-reduce(f32[3]{0:T(128)S(1)} %pad_maximum_fusion.2), channel_id=1, replica_groups=mesh['rep'=4,'fsdp'=8] {'fsdp'}, use_global_device_ids=true, to_apply=%region_8.9 | all-reduce | flops 3 | bytes 24 | tf_op jit(solution)/shard_map/psum | solution.py:57
  265.5 1.2 collective-permute-start.3
  266.7 1.2 collective-permute-done.3
  267.9 1.2 collective-permute-start.4
  269.1 1.2 collective-permute-done.4
  274.5 39.2 %all-gather.3.cloned.1.call-done = f32[1024,512]{1,0:T(8,128)} async-done(((f32[256,512]{1,0:T(8,128)}), f32[1024,512]{1,0:T(8,128)}) %all-gather.3.cloned.1.call-update) | async-done | bytes 2097168 | tf_op jit(solution)/shard_map/all_gather | solution.py:64
  313.7 1.8 fusion.3
  315.9 4.7 %fusion.1 = (bf16[1024,512]{1,0:T(8,128)(2,1)}, f32[1024,512]{1,0:T(8,128)}, f32[1024,512]{1,0:T(8,128)}, f32[1024,512]{1,0:T(8,128)}) fusion(f32[1024,512]{1,0:T(8,128)S(1)} %copy-done.2, f32[256,512]{1,0:T(8,128)S(1)} %get-tuple-element.19, f32[256,512]{1,0:T(8,128)S(1)} %get-tuple-element.20, f32[256,512]{1,0:T(8,128)S(1)} %get-tuple-element.21, ...), kind=kLoop, calls=%fused_computation.23 | loop fusion | flops 9961472 | bytes 15728640 | tf_op jit(solution)/shard_map/convert_element_type | solution.py:83
  320.6 79.9 %all-gather.5.cloned.1.call-done = bf16[8192,512]{1,0:T(8,128)(2,1)} async-done(((bf16[1024,512]{1,0:T(8,128)(2,1)}), bf16[8192,512]{1,0:T(8,128)(2,1)}) %all-gather.5.cloned.1.call-update) | async-done | bytes 8388624 | tf_op jit(solution)/shard_map/all_gather | solution.py:83
  400.5 7.3 %copy.10 = bf16[8192,512]{1,0:T(8,128)(2,1)} copy(bf16[8192,512]{1,0:T(8,128)(2,1)} %all-gather.5.cloned.1.call-done) | data formatting | bytes 16777216
  (22 shorter events, 4.5 us)
Async XLA Ops:
  7.2 1.0 copy-start
  7.2 177.8 %reduce-scatter.2.cloned.1.call-start = ((), (), s32[]{:S(2)}) async-start(), calls=%async_computation.1 | async-start | bytes 18874368 | tf_op jit(solution)/shard_map/reduce_scatter | solution.py:27
  18.4 295.2 %all-gather.3.cloned.1.call-start = ((), (), s32[]{:S(2)}) async-start(), calls=%async_computation.2 | async-start | bytes 2621440 | tf_op jit(solution)/shard_map/all_gather | solution.py:64
  185.0 25.8 %copy-start.1 = (f32[1024,512]{1,0:T(8,128)S(1)}, f32[1024,512]{1,0:T(8,128)}, u32[]{:S(2)}) copy-start(f32[1024,512]{1,0:T(8,128)} %reduce-scatter.2.cloned.1.call-done) | copy-start | bytes 6291460
  186.9 23.9 %collective-permute-start = (f32[512,512]{1,0:T(8,128)S(1)}, f32[512,512]{1,0:T(8,128)}, u32[]{:S(2)}, u32[]{:S(2)}) collective-permute-start(f32[512,512]{1,0:T(8,128)S(1)} %slice_select_fusion), channel_id=1, source_target_pairs={{0,8},{8,0},{16,24},{24,16},{1,9},{9,1},{17,25},{25,17},{2,10},{10... | collective-permute-start | bytes 3145736 | tf_op jit(solution)/shard_map/ppermute | solution.py:16
  228.9 2.7 collective-permute-start.1
  236.4 12.4 %collective-permute-start.2 = (f32[256,512]{1,0:T(8,128)S(1)}, f32[256,512]{1,0:T(8,128)S(1)}, u32[]{:S(2)}, u32[]{:S(2)}) collective-permute-start(f32[256,512]{1,0:T(8,128)S(1)} %slice_select_fusion.2), channel_id=1, source_target_pairs={{0,16},{8,24},{16,0},{24,8},{1,17},{9,25},{17,1},{25,9},{2,18},{10... | collective-permute-start | bytes 1572872 | tf_op jit(solution)/shard_map/ppermute | solution.py:16
  265.5 2.4 collective-permute-start.3
  267.9 2.4 collective-permute-start.4
  274.5 41.1 %copy-start.2 = (f32[1024,512]{1,0:T(8,128)S(1)}, f32[1024,512]{1,0:T(8,128)}, u32[]{:S(2)}) copy-start(f32[1024,512]{1,0:T(8,128)} %param.7) | copy-start | bytes 6291460
  274.5 126.1 %all-gather.5.cloned.1.call-start = ((), (), s32[]{:S(2)}) async-start(), calls=%async_computation.3 | async-start | bytes 9437184 | tf_op jit(solution)/shard_map/all_gather | solution.py:83
  313.7 2.2 copy-start.3
Sparse Core Ops, SparseCore 0:
  18.6 166.3 reduce-scatter.1
  274.6 39.0 all-gather.2
  320.8 79.7 all-gather.4
where the time goes:
time: 419 us; the launch traced here: 414 us
  waiting for transfers between devices  322 us (77%)
  blocking collectives  26.8 us (6%)
  between operations  19 us (5%)
  other arithmetic  17.1 us (4%)
  local copies, waits for them, and re-layouts  11.6 us (3%)
  matrix products  10.3 us (2%)
  starting transfers between devices  7.39 us (2%)
    reduce_scatter x1, waiting for transfers between devices, local(): lax.psum_scatter(lax.dot_general(output_grads, activations, contract_firs...  166 us
    all_gather x1, waiting for transfers between devices, local(): lax.all_gather(new_master.astype(jnp.bfloat16), 'fsdp', axis=0, tiled=True)  79.9 us
    all_gather x1, waiting for transfers between devices, local(): gathered = lax.all_gather(current, 'rep', axis=0, tiled=True)  39.2 us
    ppermute x5, waiting for transfers between devices, swapped(): lax.ppermute(shard, axis, [(i, i ^ 1 << apart) for i in range(lax.axis_si...  36.6 us
    psum x2, blocking collectives, local(): totals = lax.psum(partial_dots, 'fsdp')  26.8 us
    dot_general x1, matrix products, local(): lax.dot_general(output_grads, activations, contract_first, preferred_elem...  10.3 us
    unnamed x9, local copies, waits for them, and re-layouts  8.6 us
  transfers between devices with their start and end apart: 8, of which 8 were waited for; matrix products, arithmetic and copies ran while one was open for 0% of the time, Pallas kernels for 0%

commit v1 on v0

v1 whole, which is shorter than its diff:
```python
import functools

import jax
import jax.numpy as jnp
from jax import lax
from jax.experimental import pallas as pl
from jax.experimental.pallas import tpu as pltpu
from jax.sharding import PartitionSpec as P

dot_epsilon = 1e-06
beta_one = 0.9
beta_two = 0.95
adam_epsilon = 1e-08
learn_rate = 0.02
decay_rate = 0.1
correct_one = 1.0 - (beta_one**50) ** 2
correct_two = 1.0 - (beta_two**50) ** 2
contract_first = (((0,), (0,)), ((), ()))
MESH = pl.DeviceIdType.MESH


def drain(ref, sem):
    pltpu.make_async_copy(ref, ref, sem).wait()


def gram_pairs(count):
    return [(i, j) for i in range(count) for j in range(i, count)]


def adasum_coefs(gram, count):
    coefs = [None] * count
    members = [[i] for i in range(count)]
    scale = [1.0] * count

    def inner(left, right):
        total = 0.0
        for i in left:
            for j in right:
                total = total + scale[i] * scale[j] * gram[min(i, j), max(i, j)]
        return total

    while len(members) > 1:
        merged = []
        for left, right in zip(members[::2], members[1::2]):
            cross = inner(left, right)
            left_sq = jnp.maximum(inner(left, left), 0.0)
            right_sq = jnp.maximum(inner(right, right), 0.0)
            left_coef = 1.0 - cross / (2.0 * (left_sq + dot_epsilon))
            right_coef = 1.0 - cross / (2.0 * (right_sq + dot_epsilon))
            for i in left:
                scale[i] = left_coef * scale[i]
            for i in right:
                scale[i] = right_coef * scale[i]
            merged.append(left + right)
        members = merged
    for i in range(count):
        coefs[i] = scale[i]
    return coefs


def kernel(
    reps,
    n,
    act,
    og,
    master_in,
    first_in,
    second_in,
    master_out,
    first_out,
    second_out,
    params,
    y_all,
    x_all,
    grad,
    pieces,
    comb,
    state,
    rounded,
    dots_own,
    dots_rep,
    dots_sum,
    dots_fsdp,
    local_sem,
    own_sem,
    x_send,
    x_chain,
    x_recv,
    y_send,
    y_recv,
    p_send,
    p_recv,
    d_send,
    d_recv,
    c_send,
    c_recv,
    z_send,
    z_recv,
    w_send,
    w_recv,
    f_send,
    f_recv,
    s_send,
    s_recv,
):
    r = lax.axis_index("rep")
    f = lax.axis_index("fsdp")
    core = lax.rem(f, 2)
    chip = lax.div(f, 2)
    chips = n // 2
    sibling = chip * 2 + 1 - core
    tokens = act.shape[0]
    block = master_in.shape[0]
    piece = block // reps
    chunks, width = y_all.shape[0], y_all.shape[2]
    per_chunk = reps // chunks

    def remote(src, dst, send, recv, rep_to, fsdp_to):
        pltpu.make_async_remote_copy(
            src_ref=src,
            dst_ref=dst,
            send_sem=send,
            recv_sem=recv,
            device_id={"rep": rep_to, "fsdp": fsdp_to},
            device_id_type=MESH,
        ).start()

    def rows(start, size):
        return pl.ds(pl.multiple_of(start, 16), size)

    def chip_ahead(step):
        return lax.rem(chip + step, chips) * 2 + core

    def chip_behind(step):
        return lax.rem(chip - step + chips, chips) * 2 + core

    state_loads = [
        pltpu.make_async_copy(src, state.at[i], local_sem.at[i])
        for i, src in enumerate((master_in, first_in, second_in))
    ]
    for load in state_loads:
        load.start()
    own_x = pltpu.make_async_copy(act, x_all.at[rows(f * tokens, tokens)], local_sem.at[3])
    own_x.start()

    def own_y(s):
        column = pl.multiple_of(f * block + s * width, 128)
        return pltpu.make_async_copy(
            og.at[:, pl.ds(column, width)],
            y_all.at[s, rows(f * tokens, tokens)],
            own_sem.at[s],
        )

    for s in range(chunks):
        own_y(s).start()

    barrier = pltpu.get_barrier_semaphore()

    def greet_fsdp(step, carry):
        pl.semaphore_signal(
            barrier, inc=1, device_id={"rep": r, "fsdp": lax.rem(f + step, n)}, device_id_type=MESH
        )
        return carry

    lax.fori_loop(1, n, greet_fsdp, 0)

    def greet_rep(step, carry):
        pl.semaphore_signal(
            barrier, inc=1, device_id={"rep": lax.rem(r + step, reps), "fsdp": f}, device_id_type=MESH
        )
        return carry

    lax.fori_loop(1, reps, greet_rep, 0)
    pl.semaphore_wait(barrier, n + reps - 2)

    def x_slot(at_chip):
        return x_all.at[rows((at_chip * 2 + core) * tokens, tokens)]

    def send_x(src, slot, way, step):
        @pl.when((chip + 1 < chips) if way == 0 else (chip > 0))
        def _():
            to = (chip + 1 - 2 * way) * 2 + core
            remote(src, slot, x_send.at[way], x_chain.at[way, step], r, to)

    for way in range(2):
        send_x(act, x_slot(chip), way, 0)
    remote(act, x_slot(chip), x_send.at[2], x_recv, r, sibling)

    def place_of(s):
        return lax.rem(r + 1 + s, chunks)

    def send_y(index, carry):
        s = place_of(index // (n - 1))
        to = lax.rem(f + 1 + index % (n - 1), n)
        column = pl.multiple_of(to * block + s * width, 128)
        remote(
            og.at[:, pl.ds(column, width)],
            y_all.at[s, rows(f * tokens, tokens)],
            y_send.at[s],
            y_recv.at[s],
            r,
            to,
        )
        return carry

    early = (chunks + 1) // 2 * (n - 1)
    lax.fori_loop(0, early, send_y, 0)

    def relay_x(step, carry):
        for way in range(2):
            origin = chip - step * (1 - 2 * way)

            @pl.when((origin >= 0) if way == 0 else (origin < chips))
            def _():
                slot = x_slot(origin)
                drain(slot, x_chain.at[way, step - 1])
                send_x(slot, slot, way, step)
                remote(slot, slot, x_send.at[2], x_recv, r, sibling)

        return carry

    lax.fori_loop(1, chips, relay_x, 0)
    lax.fori_loop(early, chunks * (n - 1), send_y, 0)
    own_x.wait()
    drain(x_all.at[pl.ds(0, chips * tokens)], x_recv)

    depth = min(n * tokens, 2048)

    def chunk_sum(at_chunk, carry):
        s = place_of(at_chunk)
        own_y(s).wait()
        drain(y_all.at[s, pl.ds(0, (n - 1) * tokens)], y_recv.at[s])
        target = rows(s * width, width)
        grad[target, :] = lax.dot_general(
            y_all[s, pl.ds(0, depth), :],
            x_all[pl.ds(0, depth), :],
            contract_first,
            preferred_element_type=jnp.float32,
        )

        def more(at, inner):
            span = rows(at * depth, depth)
            grad[target, :] += lax.dot_general(
                y_all[s, span, :],
                x_all[span, :],
                contract_first,
                preferred_element_type=jnp.float32,
            )
            return inner

        lax.fori_loop(1, n * tokens // depth, more, 0)
        for sub in range(per_chunk):
            j = s * per_chunk + sub

            @pl.when(j != r)
            def _():
                remote(
                    grad.at[rows(j * piece, piece)], pieces.at[r], p_send, p_recv, j, f
                )

        return carry

    lax.fori_loop(0, chunks, chunk_sum, 0)
    pieces[r] = grad[rows(r * piece, piece), :]
    drain(pieces.at[pl.ds(0, reps - 1)], p_recv)

    pairs = gram_pairs(reps)
    lanes = 128

    def slab_dots(at, sums):
        span = pl.ds(pl.multiple_of(at * 8, 8), 8)
        parts = [pieces[i, span, :] for i in range(reps)]
        return tuple(total + parts[i] * parts[j] for total, (i, j) in zip(sums, pairs))

    zero = jnp.zeros((8, pieces.shape[2]), jnp.float32)
    sums = lax.fori_loop(0, piece // 8, slab_dots, (zero,) * len(pairs))
    dots_own[...] = jnp.zeros_like(dots_own)
    for at, total in enumerate(sums):
        line = jnp.sum(total, axis=0, keepdims=True)
        folded = line[:, 0:lanes]
        for start in range(lanes, line.shape[1], lanes):
            folded = folded + line[:, start : start + lanes]
        dots_own[at : at + 1, :] = folded

    def send_dots_rep(step, carry):
        remote(dots_own, dots_rep.at[r], d_send.at[0], d_recv.at[0], lax.rem(r + step, reps), f)
        return carry

    lax.fori_loop(1, reps, send_dots_rep, 0)
    dots_rep[r] = dots_own[...]
    drain(dots_rep.at[pl.ds(0, reps - 1)], d_recv.at[0])
    dots_sum[...] = jnp.sum(dots_rep[...], axis=0)

    def send_dots_fsdp(step, carry):
        remote(dots_sum, dots_fsdp.at[f], d_send.at[1], d_recv.at[1], r, lax.rem(f + step, n))
        return carry

    lax.fori_loop(1, n, send_dots_fsdp, 0)
    dots_fsdp[f] = dots_sum[...]
    drain(dots_fsdp.at[pl.ds(0, n - 1)], d_recv.at[1])
    dots_all = jnp.sum(jnp.sum(dots_fsdp[...], axis=0), axis=1, keepdims=True)
    features = pieces.shape[2]
    gram = {
        pair: jnp.broadcast_to(dots_all[at : at + 1, :], (1, features))
        for at, pair in enumerate(pairs)
    }
    coefs = adasum_coefs(gram, reps)

    own_rows = rows(r * piece, piece)
    for load in state_loads:
        load.wait()

    slab = 16

    def step_rows(start, combined):
        span = rows(start, slab)
        new_first = beta_one * state[1, span, :] + (1.0 - beta_one) * combined
        new_second = beta_two * state[2, span, :] + (1.0 - beta_two) * combined * combined
        update = (
            new_first / correct_one / (jnp.sqrt(new_second / correct_two) + adam_epsilon)
            + decay_rate * state[0, span, :]
        )
        new_master = state[0, span, :] - learn_rate * update
        state[0, span, :] = new_master
        state[1, span, :] = new_first
        state[2, span, :] = new_second
        rounded[span, :] = new_master.astype(jnp.bfloat16)

    def own_step(at, carry):
        span = rows(at * slab, slab)
        combined = coefs[0] * pieces[0, span, :]
        for i in range(1, reps):
            combined = combined + coefs[i] * pieces[i, span, :]
        comb[rows(r * piece + at * slab, slab), :] = combined
        return carry

    lax.fori_loop(0, piece // slab, own_step, 0)

    across = reps - 1 - r
    across_rows = rows(across * piece, piece)

    def other_reps(fn, carry):
        def body(step, inner):
            j = lax.rem(r + step, reps)

            @pl.when(j != across)
            def _():
                fn(j)

            return inner

        return lax.fori_loop(1, reps, body, carry)

    remote(comb.at[own_rows], comb.at[own_rows], c_send, c_recv.at[0], across, f)
    other_reps(
        lambda j: remote(comb.at[own_rows], comb.at[own_rows], c_send, c_recv.at[1], j, f), 0
    )

    def adam_piece(j):
        def body(at, carry):
            start = j * piece + at * slab
            step_rows(start, comb[rows(start, slab), :])
            return carry

        lax.fori_loop(0, piece // slab, body, 0)

    def send_piece(j, span, send, recv):
        def body(step, carry):
            remote(
                rounded.at[span],
                params.at[rows(f * block + j * piece, piece)],
                send,
                recv.at[step],
                r,
                chip_ahead(step),
            )
            return carry

        lax.fori_loop(1, chips, body, 0)

    adam_piece(r)
    send_piece(r, own_rows, z_send, z_recv)

    drain(comb.at[across_rows], c_recv.at[0])
    adam_piece(across)
    send_piece(across, across_rows, w_send, w_recv)

    def forward_z(step, carry):
        place = params.at[rows(chip_behind(step) * block + r * piece, piece)]
        drain(place, z_recv.at[step])
        return other_reps(lambda j: remote(place, place, f_send, f_recv.at[step], j, f), carry)

    lax.fori_loop(1, chips, forward_z, 0)

    drain(comb.at[pl.ds(0, (reps - 2) * piece)], c_recv.at[1])
    other_reps(adam_piece, 0)
    own_block = params.at[rows(f * block, block)]
    remote(rounded, own_block, s_send, s_recv, r, sibling)
    stores = [pltpu.make_async_copy(rounded, own_block, local_sem.at[3])] + [
        pltpu.make_async_copy(state.at[i], dst, local_sem.at[i])
        for i, dst in enumerate((master_out, first_out, second_out))
    ]
    for store in stores:
        store.start()

    def to_sibling(step, carry):
        start = chip_behind(step) * block
        drain(params.at[rows(start, block - 2 * piece)], f_recv.at[step])
        drain(params.at[rows(start + across * piece, piece)], w_recv.at[step])
        place = params.at[rows(start, block)]
        remote(place, place, s_send, s_recv, r, sibling)
        return carry

    lax.fori_loop(1, chips, to_sibling, 0)
    drain(params.at[pl.ds(0, chips * block)], s_recv)

    for store in stores:
        store.wait()
    drain(x_all.at[pl.ds(0, chips * tokens)], x_send.at[2])

    def drain_x(step, carry):
        @pl.when((chip + 1 < chips) & (chip >= step))
        def _():
            drain(x_slot(chip), x_send.at[0])

        @pl.when((chip > 0) & (chip + step < chips))
        def _():
            drain(x_slot(chip), x_send.at[1])

        return carry

    lax.fori_loop(0, chips - 1, drain_x, 0)

    def drain_y(s, carry):
        drain(y_all.at[s, pl.ds(0, (n - 1) * tokens)], y_send.at[s])
        return carry

    lax.fori_loop(0, chunks, drain_y, 0)
    drain(pieces.at[pl.ds(0, reps - 1)], p_send)
    drain(dots_rep.at[pl.ds(0, reps - 1)], d_send.at[0])
    drain(dots_fsdp.at[pl.ds(0, n - 1)], d_send.at[1])
    drain(comb.at[pl.ds(0, (reps - 1) * piece)], c_send)
    drain(params.at[pl.ds(0, (chips - 1) * piece)], z_send)
    drain(params.at[pl.ds(0, (chips - 1) * piece)], w_send)
    drain(params.at[pl.ds(0, (chips - 1) * (reps - 2) * piece)], f_send)
    drain(params.at[pl.ds(0, chips * block)], s_send)


def hand_out(parts, *refs):
    wide_in, params_in = refs[0:3], refs[3]
    wide_out, params_out = refs[4:7], refs[7]
    wide, narrow, in_sem, out_sem = refs[8:]
    size = params_in.shape[0] // parts
    moves = [(params_in.at[pl.ds(i * size, size)], narrow.at[i], params_out.at[pl.ds(i * size, size)]) for i in range(parts)]
    moves += [(src, wide.at[i], dst) for i, (src, dst) in enumerate(zip(wide_in, wide_out))]
    loads = [pltpu.make_async_copy(src, mid, in_sem.at[i]) for i, (src, mid, _) in enumerate(moves)]
    stores = [pltpu.make_async_copy(mid, dst, out_sem.at[i]) for i, (_, mid, dst) in enumerate(moves)]
    for load in loads:
        load.start()
    for load, store in zip(loads, stores):
        load.wait()
        store.start()
    for store in stores:
        store.wait()


def handed_out(results):
    parts = 8
    wide, params = results[0].shape, results[3].shape
    any_spec = pl.BlockSpec(memory_space=pl.ANY)
    return pl.pallas_call(
        functools.partial(hand_out, parts),
        out_shape=tuple(jax.ShapeDtypeStruct(x.shape, x.dtype) for x in results),
        in_specs=[any_spec] * 4,
        out_specs=[any_spec] * 4,
        scratch_shapes=[
            pltpu.VMEM((3, *wide), jnp.float32),
            pltpu.VMEM((parts, params[0] // parts, params[1]), jnp.bfloat16),
            pltpu.SemaphoreType.DMA((parts + 3,)),
            pltpu.SemaphoreType.DMA((parts + 3,)),
        ],
        compiler_params=pltpu.CompilerParams(vmem_limit_bytes=56 * 2**20),
    )(*results)


def local(reps, n, activations, output_grads, master, first_moment, second_moment):
    tokens, features = activations.shape
    block = master.shape[0]
    chunks = max(1, min(reps, block // 128))
    width = block // chunks
    piece = block // reps
    dot_rows = -(-len(gram_pairs(reps)) // 8) * 8
    wide = jax.ShapeDtypeStruct(master.shape, jnp.float32)
    any_spec = pl.BlockSpec(memory_space=pl.ANY)
    dma = pltpu.SemaphoreType.DMA
    results = pl.pallas_call(
        functools.partial(kernel, reps, n),
        out_shape=(
            wide,
            wide,
            wide,
            jax.ShapeDtypeStruct((n * block, features), jnp.bfloat16),
        ),
        in_specs=[any_spec] * 5,
        out_specs=[any_spec] * 4,
        scratch_shapes=[
            pltpu.VMEM((chunks, n * tokens, width), jnp.bfloat16),
            pltpu.VMEM((n * tokens, features), jnp.bfloat16),
            pltpu.VMEM((block, features), jnp.float32),
            pltpu.VMEM((reps, piece, features), jnp.float32),
            pltpu.VMEM((block, features), jnp.float32),
            pltpu.VMEM((3, block, features), jnp.float32),
            pltpu.VMEM((block, features), jnp.bfloat16),
            pltpu.VMEM((dot_rows, 128), jnp.float32),
            pltpu.VMEM((reps, dot_rows, 128), jnp.float32),
            pltpu.VMEM((dot_rows, 128), jnp.float32),
            pltpu.VMEM((n, dot_rows, 128), jnp.float32),
            dma((4,)),
            dma((chunks,)),
            dma((3,)),
            dma((2, n // 2)),
            dma,
            dma((chunks,)),
            dma((chunks,)),
            dma,
            dma,
            dma((2,)),
            dma((2,)),
            dma,
            dma((2,)),
            dma,
            dma((n // 2,)),
            dma,
            dma((n // 2,)),
            dma,
            dma((n // 2,)),
            dma,
            dma,
        ],
        compiler_params=pltpu.CompilerParams(
            collective_id=0, has_side_effects=True, vmem_limit_bytes=56 * 2**20
        ),
    )(activations, output_grads, master, first_moment, second_moment)
    return handed_out(results)


def solution(mesh):
    in_specs = (
        P(("rep", "fsdp"), None),
        P(("rep", "fsdp"), None),
        P("fsdp", None),
        P("fsdp", None),
        P("fsdp", None),
    )
    out_specs = (P("fsdp", None), P("fsdp", None), P("fsdp", None), P())
    body = functools.partial(local, mesh.shape["rep"], mesh.shape["fsdp"])
    return jax.shard_map(body, mesh=mesh, in_specs=in_specs, out_specs=out_specs, check_vma=False)
```

time: 419 us -> 184 us (0.44); the launches traced: 414 us -> 184 us
  waiting for transfers between devices: 322 us -> 0 us
  Pallas kernels: 0 us -> 183 us
  blocking collectives: 26.8 us -> 0 us
  between operations: 19 us -> 0.64 us
  other arithmetic: 17.1 us -> 0 us
  local copies, waits for them, and re-layouts: 11.6 us -> 0 us
  matrix products: 10.3 us -> 0 us
  starting transfers between devices: 7.39 us -> 0 us
    pallas_call x0 -> x2, Pallas kernels: none -> 183 us  [the longest x1 173 us: local(): pl.pallas_call(functools.partial(kernel, reps, n), out_shape=(wide, wide,...]
    reduce_scatter x1 -> x0, waiting for transfers between devices: 166 us -> none  [local(): lax.psum_scatter(lax.dot_general(output_grads, activations, contract_firs...]
    all_gather x2 -> x0, waiting for transfers between devices: 119 us -> none  [the longest x1 79.9 us: local(): lax.all_gather(new_master.astype(jnp.bfloat16), 'fsdp', axis=0, tiled=True)]
    ppermute x5 -> x0, waiting for transfers between devices: 36.6 us -> none  [swapped(): lax.ppermute(shard, axis, [(i, i ^ 1 << apart) for i in range(lax.axis_si...]
    psum x2 -> x0, blocking collectives: 26.8 us -> none  [local(): totals = lax.psum(partial_dots, 'fsdp')]
    dot_general x1 -> x0, matrix products: 10.3 us -> none  [local(): lax.dot_general(output_grads, activations, contract_first, preferred_elem...]
    unnamed x9 -> x0, local copies, waits for them, and re-layouts: 8.6 us -> none
    ppermute x5 -> x0, starting transfers between devices: 7.26 us -> none  [swapped(): lax.ppermute(shard, axis, [(i, i ^ 1 << apart) for i in range(lax.axis_si...]
  transfers between devices with their start and end apart: 8 -> 0, of which waited for: 8 -> 0; matrix products, arithmetic and copies ran while one was open for 0% -> 0% of each run, Pallas kernels for 0% -> 0%
where the time goes in v1:
time: 184 us
  Pallas kernels  183 us (99%)
    pallas_call x1, Pallas kernels, local(): pl.pallas_call(functools.partial(kernel, reps, n), out_shape=(wide, wide,...  173 us
    pallas_call x1, Pallas kernels, handed_out(): pl.pallas_call(functools.partial(hand_out, parts), out_shape=tuple((jax.S...  10.2 us

profile of v1, /device:TPU:25, one launch (start us, length us, event | category | flops | bytes accessed | tf_op | source)
XLA Modules:
  0.0 183.9 jit_solution(9338010674180752475)
XLA Ops:
  0.6 173.1 %shard_map.84 = (f32[1024,512]{1,0:T(8,128)}, f32[1024,512]{1,0:T(8,128)}, f32[1024,512]{1,0:T(8,128)}, bf16[8192,512]{1,0:T(8,128)(2,1)}) custom-call(bf16[256,512]{1,0:T(8,128)(2,1)} %act.1, bf16[256,8192]{1,0:T(8,128)(2,1)} %og.1, f32[1024,512]{1,0:T(8,128)} %master_in.1, f32[1024,512]{1,0:T(8,128)} %first_in.1, f32[1024,512]{1,0:T(8,128)} %second_in.1), custom_call_target="tpu_custom_call" | custom-call | tf_op jit(solution)/shard_map/pallas_call | solution.py:496
  173.7 10.2 %shard_map.85 = (f32[1024,512]{1,0:T(8,128)}, f32[1024,512]{1,0:T(8,128)}, f32[1024,512]{1,0:T(8,128)}, bf16[8192,512]{1,0:T(8,128)(2,1)}) custom-call(f32[1024,512]{1,0:T(8,128)} %get-tuple-element.8.refs_0_, f32[1024,512]{1,0:T(8,128)} %get-tuple-element.9.refs_1_, f32[1024,512]{1,0:T(8,128)} %get-tuple-element.10.refs_2_, ...), custom_call_target="tpu_custom_call" | custom-call | tf_op jit(solution)/shard_map/pallas_call | solution.py:471

commit v2 on v1

--- a/solution.py
+++ b/solution.py
@@ -128,12 +128,6 @@
     def rows(start, size):
         return pl.ds(pl.multiple_of(start, 16), size)
 
-    def chip_ahead(step):
-        return lax.rem(chip + step, chips) * 2 + core
-
-    def chip_behind(step):
-        return lax.rem(chip - step + chips, chips) * 2 + core
-
     state_loads = [
         pltpu.make_async_copy(src, state.at[i], local_sem.at[i])
         for i, src in enumerate((master_in, first_in, second_in))
@@ -191,7 +185,7 @@
 
     def send_y(index, carry):
         s = place_of(index // (n - 1))
-        to = lax.rem(f + 1 + index % (n - 1), n)
+        to = lax.rem(f + 1 + (index + n // 2 - 1) % (n - 1), n)
         column = pl.multiple_of(to * block + s * width, 128)
         remote(
             og.at[:, pl.ds(column, width)],
@@ -364,33 +358,61 @@
 
         lax.fori_loop(0, piece // slab, body, 0)
 
-    def send_piece(j, span, send, recv):
-        def body(step, carry):
-            remote(
-                rounded.at[span],
-                params.at[rows(f * block + j * piece, piece)],
-                send,
-                recv.at[step],
-                r,
-                chip_ahead(step),
+    def send_chain(src, dst, send, recv, step):
+        for way in range(2):
+
+            @pl.when((chip + 1 < chips) if way == 0 else (chip > 0))
+            def _():
+                to = (chip + 1 - 2 * way) * 2 + core
+                remote(src, dst, send.at[way], recv.at[way, step], r, to)
+
+    def from_each(step, fn):
+        for way in range(2):
+            origin = chip - step * (1 - 2 * way)
+
+            @pl.when((origin >= 0) if way == 0 else (origin < chips))
+            def _():
+                fn(way, origin)
+
+    def params_piece(origin, j):
+        return params.at[rows((origin * 2 + core) * block + j * piece, piece)]
+
+    def relay(j, send, recv, step, fn):
+        def one(way, origin):
+            place = params_piece(origin, j)
+            drain(place, recv.at[way, step - 1])
+
+            @pl.when((chip + 1 < chips) if way == 0 else (chip > 0))
+            def _():
+                to = (chip + 1 - 2 * way) * 2 + core
+                remote(place, place, send.at[way], recv.at[way, step], r, to)
+
+            fn(way, place)
+
+        from_each(step, one)
+
+    def relay_own(step, carry):
+        def to_reps(way, place):
+            other_reps(
+                lambda j: remote(place, place, f_send, f_recv.at[way, step - 1], j, f), 0
             )
-            return carry
-
-        lax.fori_loop(1, chips, body, 0)
+
+        relay(r, z_send, z_recv, step, to_reps)
+        return carry
+
+    def relay_across(step, carry):
+        relay(across, w_send, w_recv, step, lambda way, place: None)
+        return carry
 
     adam_piece(r)
-    send_piece(r, own_rows, z_send, z_recv)
+    send_chain(rounded.at[own_rows], params_piece(chip, r), z_send, z_recv, 0)
+    lax.fori_loop(1, min(2, chips), relay_own, 0)
 
     drain(comb.at[across_rows], c_recv.at[0])
     adam_piece(across)
-    send_piece(across, across_rows, w_send, w_recv)
-
-    def forward_z(step, carry):
-        place = params.at[rows(chip_behind(step) * block + r * piece, piece)]
-        drain(place, z_recv.at[step])
-        return other_reps(lambda j: remote(place, place, f_send, f_recv.at[step], j, f), carry)
-
-    lax.fori_loop(1, chips, forward_z, 0)
+    send_chain(rounded.at[across_rows], params_piece(chip, across), w_send, w_recv, 0)
+    lax.fori_loop(2, chips, relay_own, 0)
+    lax.fori_loop(1, min(2, chips), relay_across, 0)
 
     drain(comb.at[pl.ds(0, (reps - 2) * piece)], c_recv.at[1])
     other_reps(adam_piece, 0)
@@ -403,12 +425,15 @@
     for store in stores:
         store.start()
 
+    lax.fori_loop(2, chips, relay_across, 0)
+
     def to_sibling(step, carry):
-        start = chip_behind(step) * block
-        drain(params.at[rows(start, block - 2 * piece)], f_recv.at[step])
-        drain(params.at[rows(start + across * piece, piece)], w_recv.at[step])
-        place = params.at[rows(start, block)]
-        remote(place, place, s_send, s_recv, r, sibling)
+        def one(way, origin):
+            place = params.at[rows((origin * 2 + core) * block, block)]
+            drain(params.at[pl.ds(0, block - 2 * piece)], f_recv.at[way, step - 1])
+            remote(place, place, s_send, s_recv, r, sibling)
+
+        from_each(step, one)
         return carry
 
     lax.fori_loop(1, chips, to_sibling, 0)
@@ -418,18 +443,22 @@
         store.wait()
     drain(x_all.at[pl.ds(0, chips * tokens)], x_send.at[2])
 
-    def drain_x(step, carry):
+    def drain_chain(step, carry):
         @pl.when((chip + 1 < chips) & (chip >= step))
         def _():
             drain(x_slot(chip), x_send.at[0])
+            drain(params.at[pl.ds(0, piece)], z_send.at[0])
+            drain(params.at[pl.ds(0, piece)], w_send.at[0])
 
         @pl.when((chip > 0) & (chip + step < chips))
         def _():
             drain(x_slot(chip), x_send.at[1])
-
-        return carry
-
-    lax.fori_loop(0, chips - 1, drain_x, 0)
+            drain(params.at[pl.ds(0, piece)], z_send.at[1])
+            drain(params.at[pl.ds(0, piece)], w_send.at[1])
+
+        return carry
+
+    lax.fori_loop(0, chips - 1, drain_chain, 0)
 
     def drain_y(s, carry):
         drain(y_all.at[s, pl.ds(0, (n - 1) * tokens)], y_send.at[s])
@@ -440,8 +469,6 @@
     drain(dots_rep.at[pl.ds(0, reps - 1)], d_send.at[0])
     drain(dots_fsdp.at[pl.ds(0, n - 1)], d_send.at[1])
     drain(comb.at[pl.ds(0, (reps - 1) * piece)], c_send)
-    drain(params.at[pl.ds(0, (chips - 1) * piece)], z_send)
-    drain(params.at[pl.ds(0, (chips - 1) * piece)], w_send)
     drain(params.at[pl.ds(0, (chips - 1) * (reps - 2) * piece)], f_send)
     drain(params.at[pl.ds(0, chips * block)], s_send)
 
@@ -528,12 +555,12 @@
             dma((2,)),
             dma,
             dma((2,)),
-            dma,
-            dma((n // 2,)),
-            dma,
-            dma((n // 2,)),
-            dma,
-            dma((n // 2,)),
+            dma((2,)),
+            dma((2, n // 2)),
+            dma((2,)),
+            dma((2, n // 2)),
+            dma,
+            dma((2, n // 2)),
             dma,
             dma,
         ],

time: 184 us -> 176 us (0.957)
  Pallas kernels: 183 us -> 174 us
    pallas_call x1, Pallas kernels: 173 us -> 164 us  [local(): pl.pallas_call(functools.partial(kernel, reps, n), out_shape=(wide, wide,...]
where the time goes in v2:
time: 176 us; the launch traced here: 174 us
  Pallas kernels  174 us (99%)
    pallas_call x1, Pallas kernels, local(): pl.pallas_call(functools.partial(kernel, reps, n), out_shape=(wide, wide,...  164 us
    pallas_call x1, Pallas kernels, handed_out(): pl.pallas_call(functools.partial(hand_out, parts), out_shape=tuple((jax.S...  10.2 us

profile of v2, /device:TPU:25, one launch (start us, length us, event | category | flops | bytes accessed | tf_op | source)
XLA Modules:
  0.0 174.4 jit_solution(4950276985665662962)
XLA Ops:
  0.6 163.6 %shard_map.84 = (f32[1024,512]{1,0:T(8,128)}, f32[1024,512]{1,0:T(8,128)}, f32[1024,512]{1,0:T(8,128)}, bf16[8192,512]{1,0:T(8,128)(2,1)}) custom-call(bf16[256,512]{1,0:T(8,128)(2,1)} %act.1, bf16[256,8192]{1,0:T(8,128)(2,1)} %og.1, f32[1024,512]{1,0:T(8,128)} %master_in.1, f32[1024,512]{1,0:T(8,128)} %first_in.1, f32[1024,512]{1,0:T(8,128)} %second_in.1), custom_call_target="tpu_custom_call" | custom-call | tf_op jit(solution)/shard_map/pallas_call | solution.py:523
  164.2 10.2 %shard_map.85 = (f32[1024,512]{1,0:T(8,128)}, f32[1024,512]{1,0:T(8,128)}, f32[1024,512]{1,0:T(8,128)}, bf16[8192,512]{1,0:T(8,128)(2,1)}) custom-call(f32[1024,512]{1,0:T(8,128)} %get-tuple-element.8.refs_0_, f32[1024,512]{1,0:T(8,128)} %get-tuple-element.9.refs_1_, f32[1024,512]{1,0:T(8,128)} %get-tuple-element.10.refs_2_, ...), custom_call_target="tpu_custom_call" | custom-call | tf_op jit(solution)/shard_map/pallas_call | solution.py:498
